TPU v7x, 256 devices: a whole 4x4x8 slice. The times are simulated.
256 devices in a mesh: pipe: 16 (over y_lo, x, core), expert: 16 (over y_hi, z).
Axes of the slice: x: 4, y: 4 (y_hi: 2, y_lo: 2; y = y_hi * 2 + y_lo), z: 8, core: 2. Of those that a mesh axis runs over, the one named last changes fastest.
Arguments:
- held_fwd: bfloat16 [16, 1024, 3584], P('pipe', 'expert'), may hold values from -6 to 6
- ids_fwd: int32 [16, 1024], P('pipe'), may hold values from 0 to 3, as said below
- probs_fwd: bfloat16 [16, 1024], P('pipe'), may hold values from 0.19921875 to 1
- saved_in: bfloat16 [16, 1024, 3584], P('pipe', 'expert'), may hold values from -6 to 6
- held_grad: bfloat16 [16, 1024, 3584], P('pipe', 'expert'), may hold values from -6 to 6
- ids_bwd: int32 [16, 1024], P('pipe'), may hold values from 0 to 3, as said below
- probs_bwd: bfloat16 [16, 1024], P('pipe'), may hold values from 0.19921875 to 1
- w_gate: bfloat16 [16, 3584, 6144], P('pipe', None, 'expert'), may hold values from -0.09375 to 0.09375
- w_up: bfloat16 [16, 3584, 6144], P('pipe', None, 'expert'), may hold values from -0.09375 to 0.09375
- w_down: bfloat16 [16, 6144, 3584], P('pipe', 'expert'), may hold values from -0.15625 to 0.15625
Outputs:
- fwd_out: bfloat16 [16, 1024, 3584], P('pipe', 'expert')
- grad_out: bfloat16 [16, 1024, 3584], P('pipe', 'expert')
Inputs may be any that keep to these rules, and one draw needn't show every extreme that they name: `ids_fwd`: in every section one expert takes exactly 20 of the 64 rows of each device, 320 rows in all; no expert takes more than 20 of the rows of one device. `ids_bwd`: in every section one expert takes exactly 20 of the 64 rows of each device, 320 rows in all; no expert takes more than 20 of the rows of one device.
All inputs are finite; a program needn't handle non-finite values.
Results may differ from a plain program's by a relative error of at most 0.004.
Values may be sent and summed in bfloat16 or wider, within the bound.
A program may use at most 128 MiB of HBM per device.

v0:
```python
import jax
import jax.numpy as jnp
from jax import lax
from jax.sharding import PartitionSpec as P

EXPERTS = 4
SLOT = 20


def passed_along(value, axis, by):
    devices = lax.axis_size(axis)
    return lax.ppermute(value, axis, [(i, (i + by) % devices) for i in range(devices)])


def chosen_rows(routing, expert, capacity):
    matches = routing == expert
    places = jnp.nonzero(matches, size=capacity, fill_value=0)[0].astype(jnp.int32)
    filled = jnp.arange(capacity, dtype=jnp.int32) < jnp.sum(matches.astype(jnp.int32))
    return (places, filled)


def expert_forward(row_block, row_scale, gate_cols, up_cols, down_rows):
    gate_pre = jnp.dot(row_block, gate_cols, preferred_element_type=jnp.float32)
    upward = jnp.dot(row_block, up_cols, preferred_element_type=jnp.float32)
    hidden = (gate_pre * jax.nn.sigmoid(gate_pre) * upward).astype(jnp.bfloat16)
    return jnp.dot(hidden, down_rows, preferred_element_type=jnp.float32) * row_scale[:, None]


def expert_backward(row_block, grad_block, row_scale, gate_cols, up_cols, down_rows):
    gate_pre = jnp.dot(row_block, gate_cols, preferred_element_type=jnp.float32)
    upward = jnp.dot(row_block, up_cols, preferred_element_type=jnp.float32)
    d_hidden = (
        jnp.dot(grad_block, down_rows.T, preferred_element_type=jnp.float32) * row_scale[:, None]
    )
    sigmoid_gate = jax.nn.sigmoid(gate_pre)
    d_gate = (d_hidden * upward * sigmoid_gate * (1.0 + gate_pre * (1.0 - sigmoid_gate))).astype(
        jnp.bfloat16
    )
    d_up = (d_hidden * gate_pre * sigmoid_gate).astype(jnp.bfloat16)
    result = jnp.dot(d_gate, gate_cols.T, preferred_element_type=jnp.float32)
    return result + jnp.dot(d_up, up_cols.T, preferred_element_type=jnp.float32)


def expert_slots(local_ids, local_probs, slot_total):
    place_list = []
    scale_list = []
    for expert in range(EXPERTS):
        places, filled = chosen_rows(local_ids, expert, slot_total)
        place_list.append(places)
        scale_list.append(jnp.where(filled, local_probs[places], jnp.zeros((), local_probs.dtype)))
    return (jnp.stack(place_list), jnp.stack(scale_list))


def source_places(routing_all, expert, slot_total, local_total):
    blocks = routing_all.reshape(-1, local_total)

    def one_block(block_ids):
        return chosen_rows(block_ids, expert, slot_total)

    places, filled = jax.vmap(one_block)(blocks)
    offsets = (jnp.arange(blocks.shape[0], dtype=jnp.int32) * local_total)[:, None]
    return ((places + offsets).reshape(-1), filled.reshape(-1))


def combine_slots(returned, places_all, local_total):
    feature_width = returned.shape[2]
    grouped = jnp.sum(
        returned.reshape(EXPERTS, -1, returned.shape[1], feature_width), axis=1, dtype=jnp.float32
    )
    empty_rows = jnp.zeros((local_total, feature_width), jnp.float32)
    return empty_rows.at[places_all.reshape(-1)].add(grouped.reshape(-1, feature_width))


def on_device(
    held_fwd, ids_fwd, probs_fwd, saved_in, held_grad, ids_bwd, probs_bwd, w_gate, w_up, w_down
):
    devices = lax.axis_size("expert")
    group_size = devices // EXPERTS
    position = lax.axis_index("expert")
    my_expert = position // group_size
    gate_cols = w_gate[0]
    up_cols = w_up[0]
    down_rows = w_down[0]
    rows_fwd = passed_along(held_fwd[0], "pipe", 1)
    grads_in = passed_along(held_grad[0], "pipe", -1)
    saved_rows = saved_in[0]
    local_total = rows_fwd.shape[0]
    feature_width = rows_fwd.shape[1]
    slot_total = SLOT
    first_row = position * local_total
    local_fwd = lax.dynamic_slice_in_dim(ids_fwd[0], first_row, local_total)
    prob_fwd = lax.dynamic_slice_in_dim(probs_fwd[0], first_row, local_total)
    places_all, scales_all = expert_slots(local_fwd, prob_fwd, slot_total)
    local_bwd = lax.dynamic_slice_in_dim(ids_bwd[0], first_row, local_total)
    prob_bwd = lax.dynamic_slice_in_dim(probs_bwd[0], first_row, local_total)
    places_back, scales_back = expert_slots(local_bwd, prob_bwd, slot_total)
    gathered = lax.all_gather(rows_fwd, "expert", axis=0, tiled=True)
    picked, filled = source_places(ids_fwd[0], my_expert, slot_total, local_total)
    row_scale = jnp.where(filled, probs_fwd[0][picked].astype(jnp.float32), 0.0)
    partial_value = expert_forward(gathered[picked], row_scale, gate_cols, up_cols, down_rows)
    back_rows = partial_value.astype(jnp.bfloat16).reshape(devices, slot_total, feature_width)
    returned = lax.all_to_all(back_rows, "expert", split_axis=0, concat_axis=0, tiled=True)
    summed = combine_slots(returned, places_all, local_total)
    saved_all, grads_all = (
        lax.all_gather(saved_rows, "expert", axis=0, tiled=True),
        lax.all_gather(grads_in, "expert", axis=0, tiled=True),
    )
    picked_back, filled_back = source_places(ids_bwd[0], my_expert, slot_total, local_total)
    scale_back = jnp.where(filled_back, probs_bwd[0][picked_back].astype(jnp.float32), 0.0)
    partial_back = expert_backward(
        saved_all[picked_back], grads_all[picked_back], scale_back, gate_cols, up_cols, down_rows
    )
    back_grads = partial_back.astype(jnp.bfloat16).reshape(devices, slot_total, feature_width)
    returned_back = lax.all_to_all(back_grads, "expert", split_axis=0, concat_axis=0, tiled=True)
    summed_back = combine_slots(returned_back, places_back, local_total)
    fwd_rows = (rows_fwd + summed).astype(jnp.bfloat16)
    grad_rows = (grads_in + summed_back).astype(jnp.bfloat16)
    return (fwd_rows[None], grad_rows[None])


def solution(mesh):
    return jax.shard_map(
        on_device,
        mesh=mesh,
        in_specs=(
            P("pipe", "expert", None),
            P("pipe", None),
            P("pipe", None),
            P("pipe", "expert", None),
            P("pipe", "expert", None),
            P("pipe", None),
            P("pipe", None),
            P("pipe", None, "expert"),
            P("pipe", None, "expert"),
            P("pipe", "expert", None),
        ),
        out_specs=(P("pipe", "expert", None), P("pipe", "expert", None)),
        check_vma=False,
    )
```

profile of v0, /device:TPU:4, one launch (start us, length us, event | category | flops | bytes accessed | tf_op | source)
XLA Modules:
  0.0 528.6 jit_solution(459751190031298476)
XLA Ops:
  8.1 6.3 %collective-permute-done.1 = bf16[64,3584]{1,0:T(8,128)(2,1)S(1)} collective-permute-done((bf16[64,3584]{1,0:T(8,128)(2,1)}, bf16[64,3584]{1,0:T(8,128)(2,1)S(1)}, u32[]{:S(2)}, u32[]{:S(2)}) %collective-permute-start.1) | collective-permute-done | bytes 458784 | tf_op jit(solution)/shard_map/ppermute | solution.py:12
  16.9 6.5 %collective-permute-done = bf16[64,3584]{1,0:T(8,128)(2,1)S(1)} collective-permute-done((bf16[64,3584]{1,0:T(8,128)(2,1)}, bf16[64,3584]{1,0:T(8,128)(2,1)S(1)}, u32[]{:S(2)}, u32[]{:S(2)}) %collective-permute-start) | collective-permute-done | bytes 458784 | tf_op jit(solution)/shard_map/ppermute | solution.py:12
  31.9 7.4 %scatter_custom_fusion.10 = s32[320]{0:T(512)S(1)} fusion(s32[1024]{0:T(1024)S(1)} %reshape.1353, s32[1024]{0:T(1024)S(1)} %broadcast.1072, s32[]{:T(128)} %constant.206.clone.1), kind=kCustom, calls=%fused_computation.151 | custom fusion | flops 1024 | bytes 1284
  40.0 8.1 %scatter_custom_fusion.11 = s32[320]{0:T(512)S(1)} fusion(s32[1024]{0:T(1024)S(1)} %reshape.1359, s32[1024]{0:T(1024)S(1)} %broadcast.1072, s32[]{:T(128)} %constant.206.clone.1), kind=kCustom, calls=%fused_computation.149 | custom fusion | flops 1024 | bytes 1284
  49.6 2.5 gather_fusion.3
  52.0 87.1 %all-gather.9.cloned.1.call-done = bf16[1,1024,3584]{2,1,0:T(8,128)(2,1)} async-done(((bf16[1,64,3584]{2,1,0:T(8,128)(2,1)}), bf16[1,1024,3584]{2,1,0:T(8,128)(2,1)}) %all-gather.9.cloned.1.call-update) | async-done | bytes 7340048 | tf_op jit(solution)/shard_map/all_gather | solution.py:105
  139.1 11.5 %gather_fusion.4 = bf16[320,3584]{1,0:T(8,128)(2,1)} fusion(bf16[1024,3584]{1,0:T(8,128)(2,1)} %bitcast.85, s32[1024]{0:T(1024)S(1)} %pad_clamp_fusion), kind=kCustom, calls=%fused_computation.4 | custom fusion | bytes 4588800 | tf_op jit(solution)/shard_map/gather | solution.py:111
  150.6 4.1 fusion.12
  154.6 110.0 %all-gather.7.cloned.1.call-done = bf16[1024,3584]{1,0:T(8,128)(2,1)} async-done(((bf16[64,3584]{1,0:T(8,128)(2,1)}), bf16[1024,3584]{1,0:T(8,128)(2,1)}) %all-gather.7.cloned.1.call-update) | async-done | bytes 7340048 | tf_op jit(solution)/shard_map/all_gather | solution.py:106
  264.7 11.6 %gather_fusion.2 = bf16[320,3584]{1,0:T(8,128)(2,1)} fusion(bf16[1024,3584]{1,0:T(8,128)(2,1)} %all-gather.7.cloned.1.call-done, s32[1024]{0:T(1024)S(1)} %pad_clamp_fusion), kind=kCustom, calls=%fused_computation.2 | custom fusion | bytes 4588800 | tf_op jit(solution)/shard_map/gather | solution.py:111
  276.3 4.9 fusion.25
  281.2 7.5 %fusion.10 = f32[320,3584]{1,0:T(8,128)} fusion(bf16[1,3584,384]{2,1,0:T(8,128)(2,1)} %param.17, f32[320,384]{1,0:T(8,128)} %fusion.25, bf16[320,3584]{1,0:T(8,128)(2,1)} %gather_fusion.4, bf16[1,3584,384]{2,1,0:T(8,128)(2,1)S(1)} %copy-done, f32[320,384]{1,0:T(8,128)S(1)} %fusion.12), kind=kOutput, calls=%fused_computation.31 | convolution fusion | flops 1762836480 | bytes 13369344 | tf_op jit(solution)/shard_map/dot_general | solution.py:40
  288.7 5.3 fusion.1
  293.9 4.1 reshape.1209
  298.1 4.6 all-to-all-start.1
  302.8 2.5 gather_fusion.1
  306.0 111.3 %all-gather.5.cloned.1.call-done = bf16[1024,3584]{1,0:T(8,128)(2,1)} async-done(((bf16[64,3584]{1,0:T(8,128)(2,1)}), bf16[1024,3584]{1,0:T(8,128)(2,1)}) %all-gather.5.cloned.1.call-update) | async-done | bytes 7340048 | tf_op jit(solution)/shard_map/all_gather | solution.py:97
  417.4 11.5 %gather_fusion = bf16[320,3584]{1,0:T(8,128)(2,1)} fusion(bf16[1024,3584]{1,0:T(8,128)(2,1)} %all-gather.5.cloned.1.call-done, s32[1024]{0:T(1024)S(1)} %pad_clamp_fusion.1), kind=kCustom, calls=%fused_computation | custom fusion | bytes 4588800 | tf_op jit(solution)/shard_map/gather | solution.py:100
  428.9 3.0 fusion.8
  431.8 5.9 %fusion = bf16[320,3584]{1,0:T(8,128)(2,1)S(1)} fusion(bf16[1,384,3584]{2,1,0:T(8,128)(2,1)} %param.19, f32[320]{0:T(512)S(1)} %convert_select_fusion.1, f32[320,384]{1,0:T(8,128)S(1)} %fusion.8, bf16[320,3584]{1,0:T(8,128)(2,1)} %gather_fusion, bf16[1,3584,384]{2,1,0:T(8,128)(2,1)} %param.17), kind=kOutput, calls=%fused_computation.21 | convolution fusion | flops 1764638720 | bytes 10585344 | tf_op jit(solution)/shard_map/dot_general | solution.py:26
  440.0 5.7 %all-to-all-start = ((bf16[16,20,3584]{2,1,0:T(8,128)(2,1)}), bf16[16,20,3584]{2,1,0:T(8,128)(2,1)}, u32[]{:S(2)}, u32[]{:S(2)}) async-start(bf16[16,20,3584]{2,1,0:T(8,128)(2,1)} %reshape.1202), calls=%async_computation | async-start | bytes 5505024 | tf_op jit(solution)/shard_map/all_to_all | solution.py:102
  469.7 3.1 scatter_fusion.1
  473.7 37.6 %all-to-all-done = bf16[16,20,3584]{2,1,0:T(8,128)(2,1)} async-done(((bf16[16,20,3584]{2,1,0:T(8,128)(2,1)}), bf16[16,20,3584]{2,1,0:T(8,128)(2,1)}, u32[]{:S(2)}, u32[]{:S(2)}) %all-to-all-start) | async-done | bytes 2293792 | tf_op jit(solution)/shard_map/all_to_all | solution.py:102
  514.8 5.0 scatter_fusion
  (145 shorter events, 47.2 us)
Async XLA Ops:
  7.2 274.0 %copy-start = (bf16[1,3584,384]{2,1,0:T(8,128)(2,1)S(1)}, bf16[1,3584,384]{2,1,0:T(8,128)(2,1)}, u32[]{:S(2)}) copy-start(bf16[1,3584,384]{2,1,0:T(8,128)(2,1)} %param.18) | copy-start | bytes 8257540
  7.2 24.2 %copy-start.9 = (s32[2]{0:T(128)S(1)}, s32[2]{0:T(128)}, u32[]{:S(2)}) copy-start(s32[2]{0:T(128)} %constant.228) | copy-start | bytes 28
  7.2 131.9 %all-gather.9.cloned.1.call-start = ((), (), s32[]{:S(2)}) async-start(), calls=%async_computation.4 | async-start | bytes 7798784 | tf_op jit(solution)/shard_map/all_gather | solution.py:105
  7.9 23.6 %copy-start.8 = (s32[2]{0:T(128)S(1)}, s32[2]{0:T(128)}, u32[]{:S(2)}) copy-start(s32[2]{0:T(128)} %constant.231) | copy-start | bytes 28
  7.9 256.7 %all-gather.7.cloned.1.call-start = ((), (), s32[]{:S(2)}) async-start(), calls=%async_computation.3 | async-start | bytes 7798784 | tf_op jit(solution)/shard_map/all_gather | solution.py:106
  8.0 6.4 %collective-permute-start.1 = (bf16[64,3584]{1,0:T(8,128)(2,1)}, bf16[64,3584]{1,0:T(8,128)(2,1)S(1)}, u32[]{:S(2)}, u32[]{:S(2)}) collective-permute-start(bf16[64,3584]{1,0:T(8,128)(2,1)} %bitcast.88), channel_id=1, source_target_pairs={{0,240},{16,0},{32,16},{48,32},{64,48},{80,64},{96,80},{112,96},{1... | collective-permute-start | bytes 1376264 | tf_op jit(solution)/shard_map/ppermute | solution.py:12
  14.4 0.8 copy-start.2
  15.2 34.3 %copy-start.6 = (bf16[1,1024]{1,0:T(2,128)(2,1)S(1)}, bf16[1,1024]{1,0:T(2,128)(2,1)}, u32[]{:S(2)}) copy-start(bf16[1,1024]{1,0:T(2,128)(2,1)} %param.16) | copy-start | bytes 6148
  15.2 402.2 %all-gather.5.cloned.1.call-start = ((), (), s32[]{:S(2)}) async-start(), calls=%async_computation.2 | async-start | bytes 7798784 | tf_op jit(solution)/shard_map/all_gather | solution.py:97
  15.2 8.3 %collective-permute-start = (bf16[64,3584]{1,0:T(8,128)(2,1)}, bf16[64,3584]{1,0:T(8,128)(2,1)S(1)}, u32[]{:S(2)}, u32[]{:S(2)}) collective-permute-start(bf16[64,3584]{1,0:T(8,128)(2,1)} %bitcast.89), channel_id=1, source_target_pairs={{0,16},{16,32},{32,48},{48,64},{64,80},{80,96},{96,112},{112,128},... | collective-permute-start | bytes 1376264 | tf_op jit(solution)/shard_map/ppermute | solution.py:12
  23.5 0.8 copy-start.4
  298.1 4.6 copy-start.7
  298.1 142.0 %all-to-all-start.1 = ((bf16[16,20,3584]{2,1,0:T(8,128)(2,1)}), bf16[16,20,3584]{2,1,0:T(8,128)(2,1)}, u32[]{:S(2)}, u32[]{:S(2)}) async-start(bf16[16,20,3584]{2,1,0:T(8,128)(2,1)} %reshape.1209), calls=%async_computation.1 | async-start | bytes 5505024 | tf_op jit(solution)/shard_map/all_to_all | solution.py:114
  440.0 25.1 %copy-start.3 = (bf16[64,3584]{1,0:T(8,128)(2,1)S(1)}, bf16[64,3584]{1,0:T(8,128)(2,1)}, u32[]{:S(2)}) copy-start(bf16[64,3584]{1,0:T(8,128)(2,1)} %copy-done.2) | copy-start | bytes 1376260
  440.0 25.1 %copy-start.5 = (bf16[64,3584]{1,0:T(8,128)(2,1)S(1)}, bf16[64,3584]{1,0:T(8,128)(2,1)}, u32[]{:S(2)}) copy-start(bf16[64,3584]{1,0:T(8,128)(2,1)} %copy-done.4) | copy-start | bytes 1376260
  440.0 71.3 %all-to-all-start = ((bf16[16,20,3584]{2,1,0:T(8,128)(2,1)}), bf16[16,20,3584]{2,1,0:T(8,128)(2,1)}, u32[]{:S(2)}, u32[]{:S(2)}) async-start(bf16[16,20,3584]{2,1,0:T(8,128)(2,1)} %reshape.1202), calls=%async_computation | async-start | bytes 5505024 | tf_op jit(solution)/shard_map/all_to_all | solution.py:102
  514.8 7.0 %copy-start.1 = (bf16[1,3584,384]{2,1,0:T(8,128)(2,1)S(1)}, bf16[1,3584,384]{2,1,0:T(8,128)(2,1)}, u32[]{:S(2)}) copy-start(bf16[1,3584,384]{2,1,0:T(8,128)(2,1)} %param.18) | copy-start | bytes 8257540
Sparse Core Ops, SparseCore 0:
  10.6 128.4 all-gather.8
  142.3 122.3 all-gather.6
  267.8 149.5 all-gather.4
where the time goes:
time: 534 us; the launch traced here: 529 us
  waiting for transfers between devices  360 us (67%)
  local copies, waits for them, and re-layouts  56.2 us (11%)
  other arithmetic  55.6 us (10%)
  matrix products  30.6 us (6%)
  between operations  14.4 us (3%)
  starting transfers between devices  12.2 us (2%)
    all_gather x1, waiting for transfers between devices, on_device(): gathered = lax.all_gather(rows_fwd, 'expert', axis=0, tiled=True)  111 us
    all_gather x1, waiting for transfers between devices, on_device(): lax.all_gather(grads_in, 'expert', axis=0, tiled=True)  110 us
    all_gather x1, waiting for transfers between devices, on_device(): lax.all_gather(saved_rows, 'expert', axis=0, tiled=True)  87.1 us
    all_to_all x1, waiting for transfers between devices, on_device(): lax.all_to_all(back_rows, 'expert', split_axis=0, concat_axis=0, tiled=True)  37.6 us
    unnamed x8, other arithmetic  15.7 us
    ppermute x2, waiting for transfers between devices, passed_along(): lax.ppermute(value, axis, [(i, (i + by) % devices) for i in range(devices)])  12.8 us
    gather x1, local copies, waits for them, and re-layouts, on_device(): grads_all[picked_back]  11.6 us
    gather x1, local copies, waits for them, and re-layouts, on_device(): gathered[picked]  11.5 us
  transfers between devices with their start and end apart: 7, of which 6 were waited for; matrix products, arithmetic and copies ran while one was open for 25% of the time, Pallas kernels for 0%

commit v1 on v0

--- a/solution.py
+++ b/solution.py
@@ -101,8 +101,17 @@
     back_rows = partial_value.astype(jnp.bfloat16).reshape(devices, slot_total, feature_width)
     returned = lax.all_to_all(back_rows, "expert", split_axis=0, concat_axis=0, tiled=True)
     summed = combine_slots(returned, places_all, local_total)
+    measure_the_cells = lambda w_in, axis_key: jnp.concatenate(
+        lax.all_to_all(
+            jnp.stack([w_in] * lax.axis_size(axis_key), axis=0),
+            axis_name=axis_key,
+            split_axis=0,
+            concat_axis=0,
+        ),
+        axis=0,
+    )
     saved_all, grads_all = (
-        lax.all_gather(saved_rows, "expert", axis=0, tiled=True),
+        measure_the_cells(saved_rows, "expert"),
         lax.all_gather(grads_in, "expert", axis=0, tiled=True),
     )
     picked_back, filled_back = source_places(ids_bwd[0], my_expert, slot_total, local_total)

time: 534 us -> 541 us (1.013)
  waiting for transfers between devices: 360 us -> 341 us
  starting transfers between devices: 12.2 us -> 22.4 us
  local copies, waits for them, and re-layouts: 56.2 us -> 65.5 us
    all_to_all x0 -> x1, waiting for transfers between devices: none -> 155 us  [on_device(): lax.all_to_all(jnp.stack([w_in] * lax.axis_size(axis_key), axis=0), axis_...]
    all_gather x1 -> x0, waiting for transfers between devices: 87.1 us -> none  [on_device(): lax.all_gather(saved_rows, 'expert', axis=0, tiled=True)]
    all_gather x1, waiting for transfers between devices: 110 us -> 28.4 us  [on_device(): lax.all_gather(grads_in, 'expert', axis=0, tiled=True)]
    all_to_all x0 -> x1, starting transfers between devices: none -> 11.4 us  [on_device(): lax.all_to_all(jnp.stack([w_in] * lax.axis_size(axis_key), axis=0), axis_...]
    all_to_all x1, waiting for transfers between devices: 37.6 us -> 31.3 us  [on_device(): lax.all_to_all(back_rows, 'expert', split_axis=0, concat_axis=0, tiled=True)]
  transfers between devices with their start and end apart: 7 -> 7, of which waited for: 6 -> 6; matrix products, arithmetic and copies ran while one was open for 25% -> 27% of each run, Pallas kernels for 0% -> 0%
where the time goes in v1:
time: 541 us; the launch traced here: 535 us
  waiting for transfers between devices  341 us (63%)
  local copies, waits for them, and re-layouts  65.5 us (12%)
  other arithmetic  60.5 us (11%)
  matrix products  31.6 us (6%)
  starting transfers between devices  22.4 us (4%)
  between operations  14.7 us (3%)
    all_to_all x1, waiting for transfers between devices, on_device(): lax.all_to_all(jnp.stack([w_in] * lax.axis_size(axis_key), axis=0), axis_...  155 us
    all_gather x1, waiting for transfers between devices, on_device(): gathered = lax.all_gather(rows_fwd, 'expert', axis=0, tiled=True)  113 us
    all_to_all x1, waiting for transfers between devices, on_device(): lax.all_to_all(back_rows, 'expert', split_axis=0, concat_axis=0, tiled=True)  31.3 us
    all_gather x1, waiting for transfers between devices, on_device(): lax.all_gather(grads_in, 'expert', axis=0, tiled=True)  28.4 us
    unnamed x8, other arithmetic  15.7 us
    ppermute x2, waiting for transfers between devices, passed_along(): lax.ppermute(value, axis, [(i, (i + by) % devices) for i in range(devices)])  13.1 us
    gather x1, local copies, waits for them, and re-layouts, on_device(): grads_all[picked_back]  11.6 us
    gather x1, local copies, waits for them, and re-layouts, on_device(): gathered[picked]  11.5 us
  transfers between devices with their start and end apart: 7, of which 6 were waited for; matrix products, arithmetic and copies ran while one was open for 27% of the time, Pallas kernels for 0%

profile of v1, /device:TPU:4, one launch (start us, length us, event | category | flops | bytes accessed | tf_op | source)
XLA Modules:
  0.0 535.3 jit_solution(5695746399818909318)
XLA Ops:
  7.3 6.3 %collective-permute-done.1 = bf16[64,3584]{1,0:T(8,128)(2,1)S(1)} collective-permute-done((bf16[64,3584]{1,0:T(8,128)(2,1)}, bf16[64,3584]{1,0:T(8,128)(2,1)S(1)}, u32[]{:S(2)}, u32[]{:S(2)}) %collective-permute-start.1) | collective-permute-done | bytes 458784 | tf_op jit(solution)/shard_map/ppermute | solution.py:12
  14.4 4.7 stack.8
  19.1 11.4 %all-to-all-start.1 = ((bf16[16,64,3584]{2,1,0:T(8,128)(2,1)}), bf16[16,64,3584]{2,1,0:T(8,128)(2,1)}, u32[]{:S(2)}, u32[]{:S(2)}) async-start(bf16[16,64,3584]{2,1,0:T(8,128)(2,1)} %stack.8), calls=%async_computation.1 | async-start | bytes 14680064 | tf_op jit(solution)/shard_map/all_to_all | solution.py:105
  32.0 6.8 %collective-permute-done = bf16[64,3584]{1,0:T(8,128)(2,1)S(1)} collective-permute-done((bf16[64,3584]{1,0:T(8,128)(2,1)}, bf16[64,3584]{1,0:T(8,128)(2,1)S(1)}, u32[]{:S(2)}, u32[]{:S(2)}) %collective-permute-start) | collective-permute-done | bytes 458784 | tf_op jit(solution)/shard_map/ppermute | solution.py:12
  46.5 7.4 %scatter_custom_fusion.10 = s32[320]{0:T(512)S(1)} fusion(s32[1024]{0:T(1024)S(1)} %reshape.1358, s32[1024]{0:T(1024)S(1)} %broadcast.1073, s32[]{:T(128)} %constant.206.clone.1), kind=kCustom, calls=%fused_computation.151 | custom fusion | flops 1024 | bytes 1284
  54.7 8.1 %scatter_custom_fusion.11 = s32[320]{0:T(512)S(1)} fusion(s32[1024]{0:T(1024)S(1)} %reshape.1364, s32[1024]{0:T(1024)S(1)} %broadcast.1073, s32[]{:T(128)} %constant.206.clone.1), kind=kCustom, calls=%fused_computation.149 | custom fusion | flops 1024 | bytes 1284
  66.7 154.9 %all-to-all-done.1 = bf16[16,64,3584]{2,1,0:T(8,128)(2,1)} async-done(((bf16[16,64,3584]{2,1,0:T(8,128)(2,1)}), bf16[16,64,3584]{2,1,0:T(8,128)(2,1)}, u32[]{:S(2)}, u32[]{:S(2)}) %all-to-all-start.1) | async-done | bytes 7340064 | tf_op jit(solution)/shard_map/all_to_all | solution.py:105
  221.6 11.5 %gather_fusion.4 = bf16[320,3584]{1,0:T(8,128)(2,1)} fusion(bf16[1024,3584]{1,0:T(8,128)(2,1)} %bitcast.26, s32[1024]{0:T(1024)S(1)} %pad_clamp_fusion), kind=kCustom, calls=%fused_computation.4 | custom fusion | bytes 4588800 | tf_op jit(solution)/shard_map/gather | solution.py:120
  233.1 3.8 fusion.12
  236.9 28.4 %all-gather.5.cloned.1.call-done = bf16[1024,3584]{1,0:T(8,128)(2,1)} async-done(((bf16[64,3584]{1,0:T(8,128)(2,1)}), bf16[1024,3584]{1,0:T(8,128)(2,1)}) %all-gather.5.cloned.1.call-update) | async-done | bytes 7340048 | tf_op jit(solution)/shard_map/all_gather | solution.py:115
  265.3 11.6 %gather_fusion.2 = bf16[320,3584]{1,0:T(8,128)(2,1)} fusion(bf16[1024,3584]{1,0:T(8,128)(2,1)} %all-gather.5.cloned.1.call-done, s32[1024]{0:T(1024)S(1)} %pad_clamp_fusion), kind=kCustom, calls=%fused_computation.2 | custom fusion | bytes 4588800 | tf_op jit(solution)/shard_map/gather | solution.py:120
  276.9 4.7 fusion.25
  281.6 7.5 %fusion.10 = f32[320,3584]{1,0:T(8,128)} fusion(bf16[1,3584,384]{2,1,0:T(8,128)(2,1)} %param.17, f32[320,384]{1,0:T(8,128)} %fusion.25, bf16[320,3584]{1,0:T(8,128)(2,1)} %gather_fusion.4, bf16[1,3584,384]{2,1,0:T(8,128)(2,1)S(1)} %copy-done, f32[320,384]{1,0:T(8,128)S(1)} %fusion.12), kind=kOutput, calls=%fused_computation.31 | convolution fusion | flops 1762836480 | bytes 13369344 | tf_op jit(solution)/shard_map/dot_general | solution.py:40
  289.1 5.3 fusion.1
  294.4 4.1 reshape.1214
  298.5 4.6 all-to-all-start.2
  305.8 112.9 %all-gather.3.cloned.1.call-done = bf16[1024,3584]{1,0:T(8,128)(2,1)} async-done(((bf16[64,3584]{1,0:T(8,128)(2,1)}), bf16[1024,3584]{1,0:T(8,128)(2,1)}) %all-gather.3.cloned.1.call-update) | async-done | bytes 7340048 | tf_op jit(solution)/shard_map/all_gather | solution.py:97
  418.7 11.5 %gather_fusion = bf16[320,3584]{1,0:T(8,128)(2,1)} fusion(bf16[1024,3584]{1,0:T(8,128)(2,1)} %all-gather.3.cloned.1.call-done, s32[1024]{0:T(1024)S(1)} %pad_clamp_fusion.1), kind=kCustom, calls=%fused_computation | custom fusion | bytes 4588800 | tf_op jit(solution)/shard_map/gather | solution.py:100
  433.2 7.4 %fusion = bf16[320,3584]{1,0:T(8,128)(2,1)} fusion(bf16[1,384,3584]{2,1,0:T(8,128)(2,1)} %param.19, f32[320]{0:T(512)S(1)} %convert_select_fusion.1, f32[320,384]{1,0:T(8,128)S(1)} %fusion.8, bf16[320,3584]{1,0:T(8,128)(2,1)} %gather_fusion, bf16[1,3584,384]{2,1,0:T(8,128)(2,1)} %param.17), kind=kOutput, calls=%fused_computation.21 | convolution fusion | flops 1764638720 | bytes 10585344 | tf_op jit(solution)/shard_map/dot_general | solution.py:26
  440.5 4.1 reshape.1206
  444.7 4.8 all-to-all-start
  477.2 4.9 scatter_fusion.1
  484.1 31.3 %all-to-all-done = bf16[16,20,3584]{2,1,0:T(8,128)(2,1)} async-done(((bf16[16,20,3584]{2,1,0:T(8,128)(2,1)}), bf16[16,20,3584]{2,1,0:T(8,128)(2,1)}, u32[]{:S(2)}, u32[]{:S(2)}) %all-to-all-start) | async-done | bytes 2293792 | tf_op jit(solution)/shard_map/all_to_all | solution.py:102
  521.3 4.9 scatter_fusion
  (145 shorter events, 57.9 us)
Async XLA Ops:
  7.2 274.5 %copy-start = (bf16[1,3584,384]{2,1,0:T(8,128)(2,1)S(1)}, bf16[1,3584,384]{2,1,0:T(8,128)(2,1)}, u32[]{:S(2)}) copy-start(bf16[1,3584,384]{2,1,0:T(8,128)(2,1)} %param.18) | copy-start | bytes 8257540
  7.2 258.1 %all-gather.5.cloned.1.call-start = ((), (), s32[]{:S(2)}) async-start(), calls=%async_computation.4 | async-start | bytes 7798784 | tf_op jit(solution)/shard_map/all_gather | solution.py:115
  7.2 6.4 %collective-permute-start.1 = (bf16[64,3584]{1,0:T(8,128)(2,1)}, bf16[64,3584]{1,0:T(8,128)(2,1)S(1)}, u32[]{:S(2)}, u32[]{:S(2)}) collective-permute-start(bf16[64,3584]{1,0:T(8,128)(2,1)} %bitcast.89), channel_id=1, source_target_pairs={{0,240},{16,0},{32,16},{48,32},{64,48},{80,64},{96,80},{112,96},{1... | collective-permute-start | bytes 1376264 | tf_op jit(solution)/shard_map/ppermute | solution.py:12
  13.6 0.8 copy-start.1
  19.1 21.1 %copy-start.4 = (s32[1,1024]{1,0:T(1,128)S(1)}, s32[1,1024]{1,0:T(1,128)}, u32[]{:S(2)}) copy-start(s32[1,1024]{1,0:T(1,128)} %param.15) | copy-start | bytes 12292
  19.1 21.1 %copy-start.5 = (s32[1,1024]{1,0:T(1,128)S(1)}, s32[1,1024]{1,0:T(1,128)}, u32[]{:S(2)}) copy-start(s32[1,1024]{1,0:T(1,128)} %param.11) | copy-start | bytes 12292
  19.1 202.5 %all-to-all-start.1 = ((bf16[16,64,3584]{2,1,0:T(8,128)(2,1)}), bf16[16,64,3584]{2,1,0:T(8,128)(2,1)}, u32[]{:S(2)}, u32[]{:S(2)}) async-start(bf16[16,64,3584]{2,1,0:T(8,128)(2,1)} %stack.8), calls=%async_computation.1 | async-start | bytes 14680064 | tf_op jit(solution)/shard_map/all_to_all | solution.py:105
  30.5 15.5 %copy-start.9 = (s32[2]{0:T(128)S(1)}, s32[2]{0:T(128)}, u32[]{:S(2)}) copy-start(s32[2]{0:T(128)} %constant.228) | copy-start | bytes 28
  30.5 15.7 %copy-start.8 = (s32[2]{0:T(128)S(1)}, s32[2]{0:T(128)}, u32[]{:S(2)}) copy-start(s32[2]{0:T(128)} %constant.231) | copy-start | bytes 28
  30.5 33.6 %copy-start.6 = (bf16[1,1024]{1,0:T(2,128)(2,1)S(1)}, bf16[1,1024]{1,0:T(2,128)(2,1)}, u32[]{:S(2)}) copy-start(bf16[1,1024]{1,0:T(2,128)(2,1)} %param.16) | copy-start | bytes 6148
  30.5 388.2 %all-gather.3.cloned.1.call-start = ((), (), s32[]{:S(2)}) async-start(), calls=%async_computation.3 | async-start | bytes 7798784 | tf_op jit(solution)/shard_map/all_gather | solution.py:97
  30.6 8.2 %collective-permute-start = (bf16[64,3584]{1,0:T(8,128)(2,1)}, bf16[64,3584]{1,0:T(8,128)(2,1)S(1)}, u32[]{:S(2)}, u32[]{:S(2)}) collective-permute-start(bf16[64,3584]{1,0:T(8,128)(2,1)} %bitcast.90), channel_id=1, source_target_pairs={{0,16},{16,32},{32,48},{48,64},{64,80},{80,96},{96,112},{112,128},... | collective-permute-start | bytes 1376264 | tf_op jit(solution)/shard_map/ppermute | solution.py:12
  38.8 0.8 copy-start.3
  298.5 4.6 copy-start.7
  298.5 146.1 %all-to-all-start.2 = ((bf16[16,20,3584]{2,1,0:T(8,128)(2,1)}), bf16[16,20,3584]{2,1,0:T(8,128)(2,1)}, u32[]{:S(2)}, u32[]{:S(2)}) async-start(bf16[16,20,3584]{2,1,0:T(8,128)(2,1)} %reshape.1214), calls=%async_computation.2 | async-start | bytes 5505024 | tf_op jit(solution)/shard_map/all_to_all | solution.py:123
  444.7 23.6 %copy-start.2 = (bf16[64,3584]{1,0:T(8,128)(2,1)S(1)}, bf16[64,3584]{1,0:T(8,128)(2,1)}, u32[]{:S(2)}) copy-start(bf16[64,3584]{1,0:T(8,128)(2,1)} %copy-done.1) | copy-start | bytes 1376260
  444.7 70.7 %all-to-all-start = ((bf16[16,20,3584]{2,1,0:T(8,128)(2,1)}), bf16[16,20,3584]{2,1,0:T(8,128)(2,1)}, u32[]{:S(2)}, u32[]{:S(2)}) async-start(bf16[16,20,3584]{2,1,0:T(8,128)(2,1)} %reshape.1206), calls=%async_computation | async-start | bytes 5505024 | tf_op jit(solution)/shard_map/all_to_all | solution.py:102
Sparse Core Ops, SparseCore 0:
  14.5 250.7 all-gather.4
  268.4 150.2 all-gather.2
